TPU v7x, 32 devices: a whole 2x2x4 slice. The times are simulated.
32 devices in a mesh: dp: 8 (over z, x), mp: 4 (over y, core).
Axes of the slice: x: 2, y: 2, z: 4, core: 2. Of those that a mesh axis runs over, the one named last changes fastest.
Arguments:
- attn: bfloat16 [2, 512, 2048], P(None, 'dp', 'mp'), may hold values from -6 to 6
- resid: bfloat16 [2, 512, 4096], P(None, 'dp', 'mp'), may hold values from -6 to 6
- w_out: bfloat16 [4096, 2048], P('dp', 'mp'), may hold values from -0.125 to 0.125
- gain: float32 [4096], P('mp'), may hold values from 0.1 to 1.9
- neg_owner: int32 [512, 31], P('dp'), may hold values from 0 to 7, as said below
- neg_local: int32 [512, 31], P('dp'), may hold values from 0 to 63
Outputs:
- attn_grad: bfloat16 [2, 512, 2048], P(None, 'dp', 'mp')
- weight_grad: float32 [4096, 2048], P('dp', 'mp')
- gain_grad: float32 [4096], P('mp')
Inputs may be any that keep to these rules, and one draw needn't show every extreme that they name: `neg_owner`: among the 64 queries of one index of dp (aligned blocks of rows), no owner is named more than 496 times, and some owner exactly 496 times.
All inputs are finite; a program needn't handle non-finite values.
Results may differ from a plain program's by a relative error of at most 0.0052.
Values may be sent and summed in bfloat16 or wider, within the bound.
A program may use at most 128 MiB of HBM per device.

v0:
```python
import functools

import jax
import jax.numpy as jnp
from jax import lax
from jax.experimental import pallas as pl
from jax.experimental.pallas import tpu as pltpu
from jax.sharding import PartitionSpec as P

TAU = 0.05
LOSS_SCALE = 32.0
EPS = 1e-06


def by_query(attn, resid, w_out, gain, neg_owner, neg_local):
    groups = lax.axis_size("dp")
    pairs_here = attn.shape[1]
    feats = resid.shape[2]
    neg_count = neg_owner.shape[1]
    capacity = 2 * pairs_here * neg_count // groups
    rows_a = attn.reshape(2 * pairs_here, attn.shape[2])
    weight_full = lax.all_gather(w_out, "dp", axis=0, tiled=True)
    proj_part = lax.dot_general(
        rows_a, weight_full, (((1,), (1,)), ((), ())), preferred_element_type=jnp.float32
    )
    proj = lax.psum_scatter(proj_part, "mp", scatter_dimension=1, tiled=True)
    hidden = resid.reshape(2 * pairs_here, feats).astype(jnp.float32) + proj
    normed = hidden * gain
    squares = lax.psum(jnp.sum(normed * normed, axis=1), "mp")
    recip = lax.rsqrt(squares + EPS)[:, None]
    emb = (normed * recip).astype(jnp.bfloat16)
    query = emb[:pairs_here]
    docs = emb[pairs_here:]
    flat_owner = neg_owner.reshape(-1)
    flat_local = neg_local.reshape(-1)
    onehot = (flat_owner[:, None] == jnp.arange(groups, dtype=jnp.int32)[None, :]).astype(jnp.int32)
    ranks = jnp.sum((jnp.cumsum(onehot, axis=0) - 1) * onehot, axis=1)
    slot = flat_owner * capacity + ranks
    request = jnp.full((groups * capacity,), -1, jnp.int32).at[slot].set(flat_local)
    asked = lax.all_to_all(
        request.reshape(groups, capacity), "dp", split_axis=0, concat_axis=0, tiled=True
    )
    valid = asked >= 0
    safe_rows = jnp.maximum(asked, 0)
    outgoing = jnp.where(valid[:, :, None], docs[safe_rows], jnp.zeros((), jnp.bfloat16))
    fetched = lax.all_to_all(outgoing, "dp", split_axis=0, concat_axis=0, tiled=True)
    neg_emb = fetched.reshape(groups * capacity, feats)[slot].reshape(pairs_here, neg_count, feats)
    pos_part = jnp.sum(query.astype(jnp.float32) * docs.astype(jnp.float32), axis=1)
    neg_part = jnp.einsum("pd,pkd->pk", query, neg_emb, preferred_element_type=jnp.float32)
    partial_value = jnp.concatenate([pos_part[:, None], neg_part], axis=1)
    scores = lax.psum(partial_value, "mp") / TAU
    expo = jnp.exp(scores)
    prob = expo / jnp.sum(expo, axis=1, keepdims=True)
    first = (jnp.arange(neg_count + 1) == 0).astype(jnp.float32)[None, :]
    wts = LOSS_SCALE * (prob - first) / TAU
    query_f = query.astype(jnp.float32)
    grad_query = wts[:, 0:1] * docs.astype(jnp.float32) + jnp.einsum(
        "pk,pkd->pd", wts[:, 1:], neg_emb, preferred_element_type=jnp.float32
    )
    terms = (wts[:, 1:, None] * query_f[:, None, :]).astype(jnp.bfloat16)
    slot_buffer = (
        jnp.zeros((groups * capacity, feats), jnp.bfloat16).at[slot].set(terms.reshape(-1, feats))
    )
    returned = lax.all_to_all(
        slot_buffer.reshape(groups, capacity, feats), "dp", split_axis=0, concat_axis=0, tiled=True
    )
    targets = jnp.where(valid, asked, pairs_here).reshape(-1)
    selector = (jnp.arange(pairs_here, dtype=jnp.int32)[:, None] == targets[None, :]).astype(
        jnp.bfloat16
    )
    grad_docs = wts[:, 0:1] * query_f + jnp.dot(
        selector, returned.reshape(-1, feats), preferred_element_type=jnp.float32
    )
    demb = jnp.concatenate([grad_query, grad_docs], axis=0)
    inner = lax.psum(jnp.sum(normed * demb, axis=1), "mp")[:, None]
    dnorm = recip * demb - recip * recip * recip * normed * inner
    gain_grad = lax.psum(jnp.sum(dnorm * hidden, axis=0), "dp")
    dh = (dnorm * gain).astype(jnp.bfloat16)
    dh_full = lax.all_gather(dh, "mp", axis=1, tiled=True)
    attn_grad = (
        jnp.dot(dh_full, weight_full, preferred_element_type=jnp.float32)
        .astype(jnp.bfloat16)
        .reshape(attn.shape)
    )
    weight_grad = lax.psum_scatter(
        lax.dot_general(
            dh_full, rows_a, (((0,), (0,)), ((), ())), preferred_element_type=jnp.float32
        ),
        "dp",
        scatter_dimension=0,
        tiled=True,
    )
    return (attn_grad, weight_grad, gain_grad)


MESH = pl.DeviceIdType.MESH
BF = jnp.bfloat16
F32 = jnp.float32


def matmul(left, right, left_dim, right_dim, precision=None):
    return lax.dot_general(
        left,
        right,
        (((left_dim,), (right_dim,)), ((), ())),
        precision=precision,
        preferred_element_type=F32,
    )


def fused(
    groups,
    quarters,
    attn,
    resid,
    w_hbm,
    gain,
    owner_hbm,
    local_hbm,
    attn_grad,
    weight_grad,
    gain_grad,
    w_out,
    owner,
    local,
    rows_a,
    res_all,
    gain_all,
    proj_out,
    proj_in,
    sq_in,
    sq_all,
    dots_out,
    dots_in,
    half_out,
    half_in,
    wts_all,
    extra_in,
    extra_all,
    scale,
    gg,
    dh,
    xpart,
    xin,
    zpart,
    zin,
    load,
    zsend,
    xsend,
    arecv,
    rsend,
    rrecv,
    gsend,
    grecv,
    psend,
    precv,
    msend,
    mrecv,
    dsend,
    drecv,
    hsend,
    hrecv,
    xsend2,
    xrecv2,
    zsend2,
    zrecv2,
):
    d, m = lax.axis_index("dp"), lax.axis_index("mp")
    total = groups * quarters
    me = d * quarters + m
    here = attn.shape[1]
    pairs = groups * here
    block = w_out.shape[0] // quarters
    pair, across = m + 1 - 2 * lax.rem(m, 2), lax.rem(m + 2, quarters)
    own_rows = pairs // total
    zc, xc = d // 2, d % 2
    depth = groups // 2
    partner = zc * 2 + (1 - xc)

    def at_dp(t):
        return (t, m)

    def at_mp(t):
        return (d, t)

    def at_any(t):
        return (t // quarters, t % quarters)

    def send(src, dst, s, r, dev):
        return pltpu.make_async_remote_copy(
            src_ref=src, dst_ref=dst, send_sem=s, recv_sem=r, device_id=dev, device_id_type=MESH
        )

    def grp(s):
        return pl.ds(pl.multiple_of(s * here, here), here)

    def others(k):
        return lax.rem(me + k, total)

    barrier = pltpu.get_barrier_semaphore()

    loads = [
        pltpu.make_async_copy(attn, rows_a.at[:, grp(d), :], load.at[0]),
        pltpu.make_async_copy(w_hbm, w_out, load.at[1]),
        pltpu.make_async_copy(gain, gain_all.at[m], load.at[2]),
        pltpu.make_async_copy(owner_hbm, owner, load.at[3]),
        pltpu.make_async_copy(local_hbm, local, load.at[4]),
    ]
    for c in loads:
        c.start()

    def greet(k, c):
        pl.semaphore_signal(barrier, inc=1, device_id=at_any(others(k)), device_id_type=MESH)
        return c

    lax.fori_loop(1, total, greet, 0)
    pl.semaphore_wait(barrier, total - 1)

    pending = []
    first = send(attn, rows_a.at[:, grp(d), :], xsend.at[0], arecv.at[d], at_dp(partner))
    first.start()
    pending.append(first)
    for k in range(1, depth):
        t = lax.rem(zc + k, depth) * 2 + xc
        c = send(attn, rows_a.at[:, grp(d), :], zsend.at[k - 1], arecv.at[d], at_dp(t))
        c.start()
        pending.append(c)
    for k in range(1, quarters):
        c = send(gain, gain_all.at[m], gsend.at[k - 1], grecv.at[m], at_mp(lax.rem(m + k, quarters)))
        c.start()
        pending.append(c)

    res_sends = []
    for a in range(2):
        for j in range(quarters):
            cols = pl.ds((a * quarters + j) * block, block)
            td = 2 * m + a
            is_self = jnp.logical_and(td == d, m == j)
            c = send(
                resid.at[:, :, cols],
                res_all.at[:, grp(d), :],
                rsend.at[a * quarters + j],
                rrecv.at[d],
                (td, jnp.int32(j)),
            )
            res_sends.append((is_self, c))

            @pl.when(jnp.logical_not(is_self))
            def _(c=c):
                c.start()

            @pl.when(is_self)
            def _(cols=cols):
                c = pltpu.make_async_copy(
                    resid.at[:, :, cols], res_all.at[:, grp(d), :], load.at[5]
                )
                c.start()
                c.wait()

    def project(s, i):
        part = matmul(rows_a[:, grp(s), :].reshape(2 * here, -1), w_out[...], 1, 1)
        for j in range(quarters):
            piece = part[:, j * block : (j + 1) * block].astype(BF)
            proj_out[j, :, grp(s), :] = piece.reshape(2, here, block)
        for k in range(1, quarters):
            t = lax.rem(m + k, quarters)
            c = send(
                proj_out.at[t, :, grp(s), :],
                proj_in.at[m, :, grp(s), :],
                psend.at[k - 1, i],
                precv.at[m, s],
                at_mp(t),
            )
            c.start()
            pending.append(c)

    def wait_rows(s):
        send(attn, rows_a.at[:, grp(s), :], zsend.at[0], arecv.at[s], at_dp(partner)).wait_recv()

    loads[0].wait()
    loads[1].wait()
    project(d, 0)
    for k in range(1, depth):
        s = lax.rem(zc + depth - k, depth) * 2 + xc
        wait_rows(s)
        slot = rows_a.at[:, grp(s), :]
        c = send(slot, slot, xsend.at[k], arecv.at[s], at_dp(partner))
        c.start()
        pending.append(c)
        project(s, k)
    for k in range(depth):
        s = lax.rem(zc + depth - k, depth) * 2 + (1 - xc)
        wait_rows(s)
        project(s, depth + k)

    for c in loads[2:]:
        c.wait()
    for k in range(1, quarters):
        f = lax.rem(m + k, quarters)
        send(gain, gain_all.at[f], gsend.at[0], grecv.at[f], at_mp(f)).wait_recv()
    source = d // 2
    for s in range(groups):

        @pl.when(jnp.logical_not(jnp.logical_and(source == m, d == s)))
        def _(s=s):
            send(
                resid.at[:, :, pl.ds(0, block)],
                res_all.at[:, grp(s), :],
                rsend.at[0],
                rrecv.at[s],
                at_dp(partner),
            ).wait_recv()

    for k in range(1, quarters):
        f = lax.rem(m + k, quarters)
        for s in range(groups):
            slot = proj_in.at[f, :, grp(s), :]
            send(slot, slot, psend.at[0, 0], precv.at[f, s], at_mp(f)).wait_recv()

    proj = proj_out[m].astype(F32)
    for k in range(1, quarters):
        proj = proj + proj_in[lax.rem(m + k, quarters)].astype(F32)
    hidden = res_all[...].astype(F32) + proj
    gain_row = gain_all[source, pl.ds(lax.rem(d, 2) * quarters + m, 1), :]
    normed = hidden * gain_row
    rough = normed.astype(BF)
    squares = normed * normed
    ones = jnp.ones((8, block), F32)
    high = lax.Precision.HIGHEST
    sq_row = jnp.concatenate(
        [matmul(ones, squares[0], 1, 1, high), matmul(ones, squares[1], 1, 1, high)], axis=1
    )
    dots = matmul(rough[0], rough[1], 1, 1).astype(BF)
    dots = dots.reshape(groups, quarters, own_rows, pairs)
    for j in range(quarters):
        dots_out[j] = dots[:, j]

    def to_mp(which, src, dst):
        for k in range(1, quarters):
            t = lax.rem(m + k, quarters)
            c = send(src(t), dst.at[m], msend.at[which, k - 1], mrecv.at[which, m], at_mp(t))
            c.start()
            pending.append(c)

    def from_mp(which, dst):
        for k in range(1, quarters):
            f = lax.rem(m + k, quarters)
            slot = dst.at[f]
            send(slot, slot, msend.at[which, 0], mrecv.at[which, f], at_mp(f)).wait_recv()

    def to_dp(which, src, dst):
        for k in range(1, groups):
            t = lax.rem(d + k, groups)
            c = send(src(t), dst.at[d], dsend.at[which, k - 1], drecv.at[which, d], at_dp(t))
            c.start()
            pending.append(c)

    def from_dp(which, dst):
        for k in range(1, groups):
            f = lax.rem(d + k, groups)
            slot = dst.at[f]
            send(slot, slot, dsend.at[which, 0], drecv.at[which, f], at_dp(f)).wait_recv()

    to_mp(0, lambda t: dots_out.at[t], dots_in)
    sq_in[m] = sq_row[:1]
    to_mp(1, lambda t: sq_in.at[m], sq_in)

    mine = pl.ds(pl.multiple_of(m * own_rows, own_rows), own_rows)
    ids = owner[mine, :] * here + local[mine, :]
    column = lax.broadcasted_iota(jnp.int32, (own_rows, pairs), 1)
    row = lax.broadcasted_iota(jnp.int32, (own_rows, pairs), 0) + me * own_rows
    own = (row == column).astype(F32)
    count = jnp.zeros((own_rows, pairs), F32)
    for k in range(ids.shape[1]):
        count = count + (ids[:, k : k + 1] == column).astype(F32)

    from_mp(1, sq_in)
    sq_all[d] = jnp.sum(sq_in[...], axis=0)
    to_dp(0, lambda t: sq_all.at[d], sq_all)
    from_mp(0, dots_in)
    partial_dots = dots_out[m].astype(F32)
    for k in range(1, quarters):
        partial_dots = partial_dots + dots_in[lax.rem(m + k, quarters)].astype(F32)
    half_out[...] = partial_dots.astype(BF)
    to_dp(1, lambda t: half_out.at[t], half_in)
    from_dp(0, sq_all)
    recip = lax.rsqrt(jnp.sum(sq_all[...], axis=0) + EPS)
    scale[...] = jnp.broadcast_to(recip, (block, 2 * pairs)).T
    half_in[d] = half_out[d]
    from_dp(1, half_in)
    recip_q = scale[pl.ds(pl.multiple_of(me * own_rows, own_rows), own_rows), :][:, :1]
    cosine = jnp.sum(half_in[...].astype(F32), axis=0) * recip_q * recip[:, pairs:]
    expo = jnp.exp(cosine / TAU)
    prob = expo / jnp.sum((own + count) * expo, axis=1, keepdims=True)
    wts_neg = LOSS_SCALE * (count * prob) / TAU
    wts_pos = LOSS_SCALE * (own * (prob - 1.0)) / TAU
    along = (wts_neg + wts_pos) * cosine
    along_q = own * jnp.sum(along, axis=1, keepdims=True)
    extra_in[d] = jnp.concatenate(
        [
            jnp.sum(wts_pos, axis=0, keepdims=True),
            jnp.sum(along_q, axis=0, keepdims=True),
            jnp.sum(along, axis=0, keepdims=True),
        ],
        axis=1,
    )
    wts_all[m, d] = wts_neg.astype(BF)
    to_dp(2, lambda t: wts_all.at[m, d], wts_all.at[m])
    to_dp(3, lambda t: extra_in.at[d], extra_in)
    scaled = scale[...].reshape(2, pairs, block)
    unit = normed * scaled
    emb = unit.astype(BF)
    from_dp(2, wts_all.at[m])
    to_mp(2, lambda t: wts_all.at[m], wts_all)
    from_dp(3, extra_in)
    extra_all[m] = jnp.sum(extra_in[...], axis=0)
    to_mp(3, lambda t: extra_all.at[m], extra_all)
    from_mp(3, extra_all)
    extra = jnp.sum(extra_all[...], axis=0)
    extra = jnp.broadcast_to(extra, (block, 3 * pairs)).T
    from_mp(2, wts_all)
    wts = jnp.stack([wts_all[j] for j in range(quarters)], axis=1).reshape(pairs, pairs)
    pos = extra[:pairs]
    grad_q = matmul(wts, emb[1], 1, 0) + pos * emb[1].astype(F32)
    dn_q = scaled[0] * (grad_q - unit[0] * extra[pairs : 2 * pairs])
    here_cols = pl.ds(pl.multiple_of(m * block, block), block)
    dh[0, :, here_cols] = (dn_q * gain_row).astype(BF)

    def dh_slot(half, t):
        return dh.at[half, :, pl.ds(pl.multiple_of(t * block, block), block)]

    def send_dh(half, t, k, dev):
        slot = dh_slot(half, t)
        c = send(slot, slot, hsend.at[half, k], hrecv.at[half, t], at_mp(dev))
        c.start()
        pending.append(c)

    def wait_dh(half, t):
        slot = dh_slot(half, t)
        send(slot, slot, hsend.at[0, 0], hrecv.at[half, t], at_mp(pair)).wait_recv()

    send_dh(0, m, 0, across)
    send_dh(0, m, 1, pair)
    grad_e = matmul(wts, emb[0], 0, 0) + pos * emb[0].astype(F32)
    dn_e = scaled[1] * (grad_e - unit[1] * extra[2 * pairs :])
    dh[1, :, here_cols] = (dn_e * gain_row).astype(BF)
    send_dh(1, m, 0, across)
    send_dh(1, m, 1, pair)
    gg[m, d] = jnp.sum(dn_q * hidden[0] + dn_e * hidden[1], axis=0, keepdims=True)
    to_dp(4, lambda t: gg.at[m, d], gg.at[m])
    for half in range(2):
        wait_dh(half, across)
        send_dh(half, across, 2, pair)
    from_dp(4, gg.at[m])
    to_mp(4, lambda t: gg.at[m], gg)
    for half in range(2):
        wait_dh(half, pair)
        wait_dh(half, pair + across - m)

    def partial(s):
        rows = dh[:, grp(s), :].reshape(2 * here, -1)
        return matmul(rows, w_out[...], 1, 0).reshape(2, here, -1)

    for k in range(depth):
        tz = lax.rem(zc + 1 + k, depth)
        xpart[k] = partial(tz * 2 + (1 - xc)).astype(BF)
        c = send(xpart.at[k], xin.at[k], xsend2.at[k], xrecv2.at[k], at_dp(partner))
        c.start()
        pending.append(c)
    last = None
    for k in range(depth):
        tz = lax.rem(zc + 1 + k, depth)
        value = partial(tz * 2 + xc)
        send(xpart.at[k], xin.at[k], xsend2.at[k], xrecv2.at[k], at_dp(partner)).wait_recv()
        value = value + xin[k].astype(F32)
        if k < depth - 1:
            zpart[k] = value.astype(BF)
            c = send(zpart.at[k], zin.at[k], zsend2.at[k], zrecv2.at[k], at_dp(tz * 2 + xc))
            c.start()
            pending.append(c)
        else:
            last = value
    attn_now = last
    for j in range(quarters):
        cols = pl.ds(j * block, block)
        out = matmul(dh[0, :, cols], rows_a[0], 0, 0) + matmul(dh[1, :, cols], rows_a[1], 0, 0)
        weight_grad[j * block : (j + 1) * block, :] = out
    from_mp(4, gg)
    for a in range(2):
        for j in range(quarters):
            gain_grad[a * quarters + j] = gg[j, 2 * m + a]
    for k in range(depth - 1):
        send(zpart.at[k], zin.at[k], zsend2.at[k], zrecv2.at[k], at_dp(partner)).wait_recv()
        attn_now = attn_now + zin[k].astype(F32)
    attn_grad[...] = attn_now.astype(BF)

    for c in pending:
        c.wait_send()
    for is_self, c in res_sends:

        @pl.when(jnp.logical_not(is_self))
        def _(c=c):
            c.wait_send()


def by_feature(attn, resid, w_out, gain, neg_owner, neg_local):
    groups, quarters = lax.axis_size("dp"), lax.axis_size("mp")
    total = groups * quarters
    here = attn.shape[1]
    pairs = groups * here
    heads = attn.shape[2]
    block = w_out.shape[0] // quarters
    own_rows = pairs // total
    per = resid.shape[2] // block
    depth = groups // 2
    dma = pltpu.SemaphoreType.DMA
    vmem = pl.BlockSpec(memory_space=pltpu.VMEM)
    attn_grad, weight_grad, gain_grad = pl.pallas_call(
        functools.partial(fused, groups, quarters),
        out_shape=(
            jax.ShapeDtypeStruct(attn.shape, BF),
            jax.ShapeDtypeStruct(w_out.shape, F32),
            jax.ShapeDtypeStruct((per, 1, block), F32),
        ),
        in_specs=[pl.BlockSpec(memory_space=pltpu.HBM)] * 6,
        out_specs=(vmem,) * 3,
        scratch_shapes=[
            pltpu.VMEM(w_out.shape, BF),
            pltpu.VMEM(neg_owner.shape, jnp.int32),
            pltpu.VMEM(neg_local.shape, jnp.int32),
            pltpu.VMEM((2, pairs, heads), BF),
            pltpu.VMEM((2, pairs, block), BF),
            pltpu.VMEM((quarters, per, block), F32),
            pltpu.VMEM((quarters, 2, pairs, block), BF),
            pltpu.VMEM((quarters, 2, pairs, block), BF),
            pltpu.VMEM((quarters, 1, 2 * pairs), F32),
            pltpu.VMEM((groups, 1, 2 * pairs), F32),
            pltpu.VMEM((quarters, groups, own_rows, pairs), BF),
            pltpu.VMEM((quarters, groups, own_rows, pairs), BF),
            pltpu.VMEM((groups, own_rows, pairs), BF),
            pltpu.VMEM((groups, own_rows, pairs), BF),
            pltpu.VMEM((quarters, groups, own_rows, pairs), BF),
            pltpu.VMEM((groups, 1, 3 * pairs), F32),
            pltpu.VMEM((quarters, 1, 3 * pairs), F32),
            pltpu.VMEM((2 * pairs, block), F32),
            pltpu.VMEM((quarters, groups, 1, block), F32),
            pltpu.VMEM((2, pairs, quarters * block), BF),
            pltpu.VMEM((depth, 2, here, heads), BF),
            pltpu.VMEM((depth, 2, here, heads), BF),
            pltpu.VMEM((depth - 1, 2, here, heads), BF),
            pltpu.VMEM((depth - 1, 2, here, heads), BF),
            dma((6,)),
            dma((depth - 1,)),
            dma((depth,)),
            dma((groups,)),
            dma((per,)),
            dma((groups,)),
            dma((quarters - 1,)),
            dma((quarters,)),
            dma((quarters - 1, groups)),
            dma((quarters, groups)),
            dma((5, quarters - 1)),
            dma((5, quarters)),
            dma((5, groups - 1)),
            dma((5, groups)),
            dma((2, 3)),
            dma((2, quarters)),
            dma((depth,)),
            dma((depth,)),
            dma((depth - 1,)),
            dma((depth - 1,)),
        ],
        compiler_params=pltpu.CompilerParams(
            collective_id=0, has_side_effects=True, vmem_limit_bytes=48 * 1024 * 1024
        ),
    )(attn, resid, w_out, gain.reshape(per, block), neg_owner, neg_local)
    return attn_grad, weight_grad, gain_grad.reshape(-1)


def shards(attn, resid, w_out, gain, neg_owner, neg_local):
    groups, quarters = lax.axis_size("dp"), lax.axis_size("mp")
    here = attn.shape[1]
    block = w_out.shape[0] // quarters
    fits = quarters == 4 and block % 128 == 0 and resid.shape[2] == 2 * quarters * block and groups % 2 == 0
    fits = fits and groups * here <= 1024 and here % (16 * quarters) == 0
    plan = by_feature if fits else by_query
    return plan(attn, resid, w_out, gain, neg_owner, neg_local)


def solution(mesh):
    in_specs = (
        P(None, "dp", "mp"),
        P(None, "dp", "mp"),
        P("dp", "mp"),
        P("mp"),
        P("dp", None),
        P("dp", None),
    )
    out_specs = (P(None, "dp", "mp"), P("dp", "mp"), P("mp"))
    return jax.shard_map(shards, mesh=mesh, in_specs=in_specs, out_specs=out_specs, check_vma=False)
```

profile of v0, /device:TPU:0, one launch (start us, length us, event | category | flops | bytes accessed | tf_op | source)
XLA Modules:
  0.0 97.3 jit_solution(12449996895778045979)
XLA Ops:
  0.6 0.0 copy-start.4
  0.6 0.8 copy.9.owner_hbm
  1.4 0.0 copy-done.4
  1.4 0.0 copy-start.3
  1.5 0.1 copy.10.local_hbm
  1.6 0.6 copy-done.3
  2.1 0.0 copy-start
  2.1 1.0 %copy-done = bf16[512,512]{1,0:T(8,128)(2,1)S(1)} copy-done((bf16[512,512]{1,0:T(8,128)(2,1)S(1)}, bf16[512,512]{1,0:T(8,128)(2,1)}, u32[]{:S(2)}) %copy-start) | copy-done | bytes 524312
  3.2 0.0 copy-start.1
  3.2 0.9 copy-done.1
  4.1 0.0 copy-start.2
  4.1 0.9 copy-done.2
  5.0 90.0 %shard_map.85 = (bf16[2,64,512]{2,1,0:T(8,128)(2,1)S(1)}, f32[512,512]{1,0:T(8,128)S(1)}, f32[8,1,128]{2,1,0:T(1,128)S(1)}) custom-call(bf16[2,64,512]{2,1,0:T(8,128)(2,1)S(1)} %copy-done.2, bf16[2,64,1024]{2,1,0:T(8,128)(2,1)S(1)} %copy-done.1, bf16[512,512]{1,0:T(8,128)(2,1)S(1)} %copy-done, f32[8,128]{1,0:T(8,128)S(1)} %bitcast.2, ...), custom_call_target="tpu_custom_call" | custom-call | tf_op jit(solution)/shard_map/pallas_call | solution.py:518
  95.1 0.7 copy.14
  95.7 1.0 copy.15
  96.7 0.6 copy.16
Async XLA Ops:
  0.6 0.8 copy-start.4
  1.4 0.7 copy-start.3
  2.1 1.0 %copy-start = (bf16[512,512]{1,0:T(8,128)(2,1)S(1)}, bf16[512,512]{1,0:T(8,128)(2,1)}, u32[]{:S(2)}) copy-start(bf16[512,512]{1,0:T(8,128)(2,1)} %w_hbm.1) | copy-start | bytes 1572868
  3.2 0.9 copy-start.1
  4.1 0.9 copy-start.2
where the time goes:
time: 98.3 us; the launch traced here: 97.3 us
  Pallas kernels  90 us (92%)
  local copies, waits for them, and re-layouts  6.61 us (7%)
    pallas_call x1, Pallas kernels, by_feature(): pl.pallas_call(functools.partial(fused, groups, quarters), out_shape=(jax...  90 us
    unnamed x15, local copies, waits for them, and re-layouts  6.61 us

commit v1 on v0

--- a/solution.py
+++ b/solution.py
@@ -220,11 +220,17 @@
     first = send(attn, rows_a.at[:, grp(d), :], xsend.at[0], arecv.at[d], at_dp(partner))
     first.start()
     pending.append(first)
-    for k in range(1, depth):
-        t = lax.rem(zc + k, depth) * 2 + xc
-        c = send(attn, rows_a.at[:, grp(d), :], zsend.at[k - 1], arecv.at[d], at_dp(t))
-        c.start()
-        pending.append(c)
+    middle = (zc + 1) // 2 == 1
+    near = zc + 1 - 2 * lax.rem(zc, 2)
+    c = send(attn, rows_a.at[:, grp(d), :], zsend.at[0], arecv.at[d], at_dp(near * 2 + xc))
+    c.start()
+    pending.append(c)
+    passed = [send(attn, rows_a.at[:, grp(d), :], zsend.at[1], arecv.at[d], at_dp((3 - zc) * 2 + xc))]
+
+    @pl.when(middle)
+    def _():
+        passed[0].start()
+
     for k in range(1, quarters):
         c = send(gain, gain_all.at[m], gsend.at[k - 1], grecv.at[m], at_mp(lax.rem(m + k, quarters)))
         c.start()
@@ -280,16 +286,26 @@
     loads[0].wait()
     loads[1].wait()
     project(d, 0)
+    half = zc // 2
+    nearest = (near, 2 - half, 3 - 3 * half)
     for k in range(1, depth):
-        s = lax.rem(zc + depth - k, depth) * 2 + xc
+        s = nearest[k - 1] * 2 + xc
+        onward = 3 - zc if k == 1 else 3 * (zc - 1)
         wait_rows(s)
         slot = rows_a.at[:, grp(s), :]
+        c = send(slot, slot, zsend.at[k + 1], arecv.at[s], at_dp(onward * 2 + xc))
+        passed.append(c)
+
+        @pl.when(middle)
+        def _(c=c):
+            c.start()
+
         c = send(slot, slot, xsend.at[k], arecv.at[s], at_dp(partner))
         c.start()
         pending.append(c)
         project(s, k)
     for k in range(depth):
-        s = lax.rem(zc + depth - k, depth) * 2 + (1 - xc)
+        s = (zc if k == 0 else nearest[k - 1]) * 2 + (1 - xc)
         wait_rows(s)
         project(s, depth + k)
 
@@ -324,12 +340,6 @@
     gain_row = gain_all[source, pl.ds(lax.rem(d, 2) * quarters + m, 1), :]
     normed = hidden * gain_row
     rough = normed.astype(BF)
-    squares = normed * normed
-    ones = jnp.ones((8, block), F32)
-    high = lax.Precision.HIGHEST
-    sq_row = jnp.concatenate(
-        [matmul(ones, squares[0], 1, 1, high), matmul(ones, squares[1], 1, 1, high)], axis=1
-    )
     dots = matmul(rough[0], rough[1], 1, 1).astype(BF)
     dots = dots.reshape(groups, quarters, own_rows, pairs)
     for j in range(quarters):
@@ -362,6 +372,12 @@
             send(slot, slot, dsend.at[which, 0], drecv.at[which, f], at_dp(f)).wait_recv()
 
     to_mp(0, lambda t: dots_out.at[t], dots_in)
+    squares = normed * normed
+    ones = jnp.ones((8, block), F32)
+    high = lax.Precision.HIGHEST
+    sq_row = jnp.concatenate(
+        [matmul(ones, squares[0], 1, 1, high), matmul(ones, squares[1], 1, 1, high)], axis=1
+    )
     sq_in[m] = sq_row[:1]
     to_mp(1, lambda t: sq_in.at[m], sq_in)
 
@@ -496,6 +512,12 @@
 
     for c in pending:
         c.wait_send()
+    for c in passed:
+
+        @pl.when(middle)
+        def _(c=c):
+            c.wait_send()
+
     for is_self, c in res_sends:
 
         @pl.when(jnp.logical_not(is_self))
@@ -550,7 +572,7 @@
             pltpu.VMEM((depth - 1, 2, here, heads), BF),
             pltpu.VMEM((depth - 1, 2, here, heads), BF),
             dma((6,)),
-            dma((depth - 1,)),
+            dma((depth + 1,)),
             dma((depth,)),
             dma((groups,)),
             dma((per,)),
@@ -571,7 +593,7 @@
             dma((depth - 1,)),
         ],
         compiler_params=pltpu.CompilerParams(
-            collective_id=0, has_side_effects=True, vmem_limit_bytes=48 * 1024 * 1024
+            collective_id=0, has_side_effects=True, vmem_limit_bytes=60 * 1024 * 1024
         ),
     )(attn, resid, w_out, gain.reshape(per, block), neg_owner, neg_local)
     return attn_grad, weight_grad, gain_grad.reshape(-1)
@@ -581,7 +603,7 @@
     groups, quarters = lax.axis_size("dp"), lax.axis_size("mp")
     here = attn.shape[1]
     block = w_out.shape[0] // quarters
-    fits = quarters == 4 and block % 128 == 0 and resid.shape[2] == 2 * quarters * block and groups % 2 == 0
+    fits = quarters == 4 and groups == 8 and block % 128 == 0 and resid.shape[2] == 2 * quarters * block
     fits = fits and groups * here <= 1024 and here % (16 * quarters) == 0
     plan = by_feature if fits else by_query
     return plan(attn, resid, w_out, gain, neg_owner, neg_local)

time: 98.3 us -> 102 us (1.038)
  Pallas kernels: 90 us -> 94 us
    pallas_call x1, Pallas kernels: 90 us -> 94 us  [by_feature(): pl.pallas_call(functools.partial(fused, groups, quarters), out_shape=(jax...]
    unnamed x15 -> x9, local copies, waits for them, and re-layouts: 6.61 us -> 6.56 us
where the time goes in v1:
time: 102 us; the launch traced here: 101 us
  Pallas kernels  94 us (92%)
  local copies, waits for them, and re-layouts  6.56 us (6%)
    pallas_call x1, Pallas kernels, by_feature(): pl.pallas_call(functools.partial(fused, groups, quarters), out_shape=(jax...  94 us
    unnamed x9, local copies, waits for them, and re-layouts  6.56 us

profile of v1, /device:TPU:0, one launch (start us, length us, event | category | flops | bytes accessed | tf_op | source)
XLA Modules:
  0.0 101.2 jit_solution(6055479001228186299)
XLA Ops:
  0.6 0.0 copy-start
  0.6 1.4 %copy.9.owner_hbm = s32[64,31]{1,0:T(8,128)} copy(s32[64,31]{0,1:T(8,128)} %param.10) | data formatting | bytes 15872 | tf_op args[4]
  2.1 0.0 copy-done
  2.1 0.7 copy.10.local_hbm
  2.8 94.0 %shard_map.85 = (bf16[2,64,512]{2,1,0:T(8,128)(2,1)}, f32[512,512]{1,0:T(8,128)}, f32[8,1,128]{2,1,0:T(1,128)}) custom-call(bf16[2,64,512]{2,1,0:T(8,128)(2,1)} %attn.1, bf16[2,64,1024]{2,1,0:T(8,128)(2,1)} %resid.1, bf16[512,512]{1,0:T(8,128)(2,1)} %w_hbm.1, f32[8,128]{1,0:T(8,128)} %bitcast.2, s32[64,31]{1,0:T(8,128)} %copy.9.owner_hbm, ...), custom_call_target="tpu_custom_call" | custom-call | tf_op jit(solution)/shard_map/pallas_call | solution.py:540
  96.8 1.6 %copy.14 = bf16[2,64,512]{2,1,0:T(8,128)(2,1)} copy(bf16[2,64,512]{2,1,0:T(8,128)(2,1)} %get-tuple-element.12) | data formatting | bytes 262144
  98.4 0.0 copy-start.1
  98.4 2.3 %copy.15 = f32[512,512]{1,0:T(8,128)} copy(f32[512,512]{1,0:T(8,128)} %get-tuple-element.13) | data formatting | bytes 2097152
  100.7 0.0 copy-done.1
  100.7 0.6 copy.16
Async XLA Ops:
  0.6 1.4 %copy-start = (s32[64,31]{0,1:T(8,128)S(1)}, s32[64,31]{0,1:T(8,128)}, u32[]{:S(2)}) copy-start(s32[64,31]{0,1:T(8,128)} %param.11) | copy-start | bytes 23812
  98.4 2.3 %copy-start.1 = (f32[8,1,128]{2,1,0:T(1,128)S(1)}, f32[8,1,128]{2,1,0:T(1,128)}, u32[]{:S(2)}) copy-start(f32[8,1,128]{2,1,0:T(1,128)} %get-tuple-element.8) | copy-start | bytes 12292

commit v2 on v1

--- a/solution.py
+++ b/solution.py
@@ -98,12 +98,11 @@
 F32 = jnp.float32
 
 
-def matmul(left, right, left_dim, right_dim, precision=None):
+def matmul(left, right, left_dim, right_dim):
     return lax.dot_general(
         left,
         right,
         (((left_dim,), (right_dim,)), ((), ())),
-        precision=precision,
         preferred_element_type=F32,
     )
 
@@ -140,6 +139,7 @@
     scale,
     gg,
     dh,
+    part,
     xpart,
     xin,
     zpart,
@@ -373,10 +373,11 @@
 
     to_mp(0, lambda t: dots_out.at[t], dots_in)
     squares = normed * normed
-    ones = jnp.ones((8, block), F32)
-    high = lax.Precision.HIGHEST
+    ones = jnp.ones((16, block), BF)
+    upper = squares.astype(BF)
+    lower = (squares - upper.astype(F32)).astype(BF)
     sq_row = jnp.concatenate(
-        [matmul(ones, squares[0], 1, 1, high), matmul(ones, squares[1], 1, 1, high)], axis=1
+        [matmul(ones, upper[h], 1, 1) + matmul(ones, lower[h], 1, 1) for h in range(2)], axis=1
     )
     sq_in[m] = sq_row[:1]
     to_mp(1, lambda t: sq_in.at[m], sq_in)
@@ -464,51 +465,56 @@
     send_dh(1, m, 1, pair)
     gg[m, d] = jnp.sum(dn_q * hidden[0] + dn_e * hidden[1], axis=0, keepdims=True)
     to_dp(4, lambda t: gg.at[m, d], gg.at[m])
+    order = [lax.rem(zc + 1 + k, depth) for k in range(depth)]
+
+    def x_copy(half, k):
+        slot = (half, order[k])
+        return send(
+            xpart.at[slot], xin.at[slot], xsend2.at[slot], xrecv2.at[slot], at_dp(partner)
+        )
+
+    def z_copy(half, k):
+        slot = (half, k)
+        dev = at_dp(order[k] * 2 + xc)
+        return send(zpart.at[slot], zin.at[slot], zsend2.at[slot], zrecv2.at[slot], dev)
+
     for half in range(2):
         wait_dh(half, across)
         send_dh(half, across, 2, pair)
+        wait_dh(half, pair)
+        wait_dh(half, pair + across - m)
+        part[half] = matmul(dh[half], w_out[...], 1, 0).reshape(depth, 2, here, -1)
+        xpart[half] = part[half, :, 1 - xc].astype(BF)
+        for k in range(depth):
+            c = x_copy(half, k)
+            c.start()
+            pending.append(c)
     from_dp(4, gg.at[m])
     to_mp(4, lambda t: gg.at[m], gg)
+    weight_grad[...] = matmul(dh[0], rows_a[0], 0, 0)
+    attn_now = []
     for half in range(2):
-        wait_dh(half, pair)
-        wait_dh(half, pair + across - m)
-
-    def partial(s):
-        rows = dh[:, grp(s), :].reshape(2 * here, -1)
-        return matmul(rows, w_out[...], 1, 0).reshape(2, here, -1)
-
-    for k in range(depth):
-        tz = lax.rem(zc + 1 + k, depth)
-        xpart[k] = partial(tz * 2 + (1 - xc)).astype(BF)
-        c = send(xpart.at[k], xin.at[k], xsend2.at[k], xrecv2.at[k], at_dp(partner))
-        c.start()
-        pending.append(c)
-    last = None
-    for k in range(depth):
-        tz = lax.rem(zc + 1 + k, depth)
-        value = partial(tz * 2 + xc)
-        send(xpart.at[k], xin.at[k], xsend2.at[k], xrecv2.at[k], at_dp(partner)).wait_recv()
-        value = value + xin[k].astype(F32)
-        if k < depth - 1:
-            zpart[k] = value.astype(BF)
-            c = send(zpart.at[k], zin.at[k], zsend2.at[k], zrecv2.at[k], at_dp(tz * 2 + xc))
-            c.start()
-            pending.append(c)
-        else:
-            last = value
-    attn_now = last
-    for j in range(quarters):
-        cols = pl.ds(j * block, block)
-        out = matmul(dh[0, :, cols], rows_a[0], 0, 0) + matmul(dh[1, :, cols], rows_a[1], 0, 0)
-        weight_grad[j * block : (j + 1) * block, :] = out
+        for k in range(depth):
+            x_copy(half, k).wait_recv()
+            value = part[half, order[k], xc] + xin[half, order[k]].astype(F32)
+            if k < depth - 1:
+                zpart[half, k] = value.astype(BF)
+                c = z_copy(half, k)
+                c.start()
+                pending.append(c)
+            else:
+                attn_now.append(value)
+    weight_grad[...] += matmul(dh[1], rows_a[1], 0, 0)
     from_mp(4, gg)
     for a in range(2):
         for j in range(quarters):
             gain_grad[a * quarters + j] = gg[j, 2 * m + a]
-    for k in range(depth - 1):
-        send(zpart.at[k], zin.at[k], zsend2.at[k], zrecv2.at[k], at_dp(partner)).wait_recv()
-        attn_now = attn_now + zin[k].astype(F32)
-    attn_grad[...] = attn_now.astype(BF)
+    for half in range(2):
+        value = attn_now[half]
+        for k in range(depth - 1):
+            z_copy(half, k).wait_recv()
+            value = value + zin[half, k].astype(F32)
+        attn_grad[half] = value.astype(BF)
 
     for c in pending:
         c.wait_send()
@@ -567,10 +573,11 @@
             pltpu.VMEM((2 * pairs, block), F32),
             pltpu.VMEM((quarters, groups, 1, block), F32),
             pltpu.VMEM((2, pairs, quarters * block), BF),
-            pltpu.VMEM((depth, 2, here, heads), BF),
-            pltpu.VMEM((depth, 2, here, heads), BF),
-            pltpu.VMEM((depth - 1, 2, here, heads), BF),
-            pltpu.VMEM((depth - 1, 2, here, heads), BF),
+            pltpu.VMEM((2, depth, 2, here, heads), F32),
+            pltpu.VMEM((2, depth, here, heads), BF),
+            pltpu.VMEM((2, depth, here, heads), BF),
+            pltpu.VMEM((2, depth - 1, here, heads), BF),
+            pltpu.VMEM((2, depth - 1, here, heads), BF),
             dma((6,)),
             dma((depth + 1,)),
             dma((depth,)),
@@ -587,13 +594,13 @@
             dma((5, groups)),
             dma((2, 3)),
             dma((2, quarters)),
-            dma((depth,)),
-            dma((depth,)),
-            dma((depth - 1,)),
-            dma((depth - 1,)),
+            dma((2, depth)),
+            dma((2, depth)),
+            dma((2, depth - 1)),
+            dma((2, depth - 1)),
         ],
         compiler_params=pltpu.CompilerParams(
-            collective_id=0, has_side_effects=True, vmem_limit_bytes=60 * 1024 * 1024
+            collective_id=0, has_side_effects=True, vmem_limit_bytes=48 * 1024 * 1024
         ),
     )(attn, resid, w_out, gain.reshape(per, block), neg_owner, neg_local)
     return attn_grad, weight_grad, gain_grad.reshape(-1)

time: 102 us -> 96.4 us (0.945)
  Pallas kernels: 94 us -> 88.8 us
    pallas_call x1, Pallas kernels: 94 us -> 88.8 us  [by_feature(): pl.pallas_call(functools.partial(fused, groups, quarters), out_shape=(jax...]
    unnamed x9 -> x15, local copies, waits for them, and re-layouts: 6.56 us -> 6.61 us
where the time goes in v2:
time: 96.4 us; the launch traced here: 96.1 us
  Pallas kernels  88.8 us (92%)
  local copies, waits for them, and re-layouts  6.61 us (7%)
    pallas_call x1, Pallas kernels, by_feature(): pl.pallas_call(functools.partial(fused, groups, quarters), out_shape=(jax...  88.8 us
    unnamed x15, local copies, waits for them, and re-layouts  6.61 us

profile of v2, /device:TPU:0, one launch (start us, length us, event | category | flops | bytes accessed | tf_op | source)
XLA Modules:
  0.0 96.1 jit_solution(13888213688777806141)
XLA Ops:
  0.6 0.0 copy-start.4
  0.6 0.8 copy.9.owner_hbm
  1.4 0.0 copy-done.4
  1.4 0.0 copy-start.3
  1.5 0.1 copy.10.local_hbm
  1.6 0.6 copy-done.3
  2.1 0.0 copy-start
  2.1 1.0 %copy-done = bf16[512,512]{1,0:T(8,128)(2,1)S(1)} copy-done((bf16[512,512]{1,0:T(8,128)(2,1)S(1)}, bf16[512,512]{1,0:T(8,128)(2,1)}, u32[]{:S(2)}) %copy-start) | copy-done | bytes 524312
  3.2 0.0 copy-start.1
  3.2 0.9 copy-done.1
  4.1 0.0 copy-start.2
  4.1 0.9 copy-done.2
  5.0 88.8 %shard_map.85 = (bf16[2,64,512]{2,1,0:T(8,128)(2,1)S(1)}, f32[512,512]{1,0:T(8,128)S(1)}, f32[8,1,128]{2,1,0:T(1,128)S(1)}) custom-call(bf16[2,64,512]{2,1,0:T(8,128)(2,1)S(1)} %copy-done.2, bf16[2,64,1024]{2,1,0:T(8,128)(2,1)S(1)} %copy-done.1, bf16[512,512]{1,0:T(8,128)(2,1)S(1)} %copy-done, f32[8,128]{1,0:T(8,128)S(1)} %bitcast.2, ...), custom_call_target="tpu_custom_call" | custom-call | tf_op jit(solution)/shard_map/pallas_call | solution.py:546
  93.8 0.7 copy.14
  94.5 1.0 %copy.15 = f32[512,512]{1,0:T(8,128)} copy(f32[512,512]{1,0:T(8,128)S(1)} %get-tuple-element.13) | data formatting | bytes 2097152
  95.5 0.6 copy.16
Async XLA Ops:
  0.6 0.8 copy-start.4
  1.4 0.7 copy-start.3
  2.1 1.0 %copy-start = (bf16[512,512]{1,0:T(8,128)(2,1)S(1)}, bf16[512,512]{1,0:T(8,128)(2,1)}, u32[]{:S(2)}) copy-start(bf16[512,512]{1,0:T(8,128)(2,1)} %w_hbm.1) | copy-start | bytes 1572868
  3.2 0.9 copy-start.1
  4.1 0.9 copy-start.2

commit v3 on v2

--- a/solution.py
+++ b/solution.py
@@ -114,14 +114,12 @@
     resid,
     w_hbm,
     gain,
-    owner_hbm,
-    local_hbm,
+    ids_hbm,
     attn_grad,
     weight_grad,
     gain_grad,
     w_out,
-    owner,
-    local,
+    ids_here,
     rows_a,
     res_all,
     gain_all,
@@ -203,8 +201,7 @@
         pltpu.make_async_copy(attn, rows_a.at[:, grp(d), :], load.at[0]),
         pltpu.make_async_copy(w_hbm, w_out, load.at[1]),
         pltpu.make_async_copy(gain, gain_all.at[m], load.at[2]),
-        pltpu.make_async_copy(owner_hbm, owner, load.at[3]),
-        pltpu.make_async_copy(local_hbm, local, load.at[4]),
+        pltpu.make_async_copy(ids_hbm, ids_here, load.at[3]),
     ]
     for c in loads:
         c.start()
@@ -383,7 +380,7 @@
     to_mp(1, lambda t: sq_in.at[m], sq_in)
 
     mine = pl.ds(pl.multiple_of(m * own_rows, own_rows), own_rows)
-    ids = owner[mine, :] * here + local[mine, :]
+    ids = ids_here[mine, :]
     column = lax.broadcasted_iota(jnp.int32, (own_rows, pairs), 1)
     row = lax.broadcasted_iota(jnp.int32, (own_rows, pairs), 0) + me * own_rows
     own = (row == column).astype(F32)
@@ -428,14 +425,29 @@
     unit = normed * scaled
     emb = unit.astype(BF)
     from_dp(2, wts_all.at[m])
-    to_mp(2, lambda t: wts_all.at[m], wts_all)
+
+    def pass_wts(t, k, dev):
+        slot = wts_all.at[t]
+        c = send(slot, slot, msend.at[2, k], mrecv.at[2, t], at_mp(dev))
+        c.start()
+        pending.append(c)
+
+    def wait_wts(t):
+        slot = wts_all.at[t]
+        send(slot, slot, msend.at[2, 0], mrecv.at[2, t], at_mp(pair)).wait_recv()
+
+    pass_wts(m, 0, across)
+    pass_wts(m, 1, pair)
     from_dp(3, extra_in)
     extra_all[m] = jnp.sum(extra_in[...], axis=0)
     to_mp(3, lambda t: extra_all.at[m], extra_all)
+    wait_wts(across)
+    pass_wts(across, 2, pair)
     from_mp(3, extra_all)
     extra = jnp.sum(extra_all[...], axis=0)
     extra = jnp.broadcast_to(extra, (block, 3 * pairs)).T
-    from_mp(2, wts_all)
+    wait_wts(pair)
+    wait_wts(pair + across - m)
     wts = jnp.stack([wts_all[j] for j in range(quarters)], axis=1).reshape(pairs, pairs)
     pos = extra[:pairs]
     grad_q = matmul(wts, emb[1], 1, 0) + pos * emb[1].astype(F32)
@@ -550,12 +562,11 @@
             jax.ShapeDtypeStruct(w_out.shape, F32),
             jax.ShapeDtypeStruct((per, 1, block), F32),
         ),
-        in_specs=[pl.BlockSpec(memory_space=pltpu.HBM)] * 6,
+        in_specs=[pl.BlockSpec(memory_space=pltpu.HBM)] * 5,
         out_specs=(vmem,) * 3,
         scratch_shapes=[
             pltpu.VMEM(w_out.shape, BF),
             pltpu.VMEM(neg_owner.shape, jnp.int32),
-            pltpu.VMEM(neg_local.shape, jnp.int32),
             pltpu.VMEM((2, pairs, heads), BF),
             pltpu.VMEM((2, pairs, block), BF),
             pltpu.VMEM((quarters, per, block), F32),
@@ -602,7 +613,7 @@
         compiler_params=pltpu.CompilerParams(
             collective_id=0, has_side_effects=True, vmem_limit_bytes=48 * 1024 * 1024
         ),
-    )(attn, resid, w_out, gain.reshape(per, block), neg_owner, neg_local)
+    )(attn, resid, w_out, gain.reshape(per, block), neg_owner * here + neg_local)
     return attn_grad, weight_grad, gain_grad.reshape(-1)
 
 

time: 96.4 us -> 95.2 us (0.988)
  Pallas kernels: 88.8 us -> 87.6 us
    pallas_call x1, Pallas kernels: 88.8 us -> 87.6 us  [by_feature(): pl.pallas_call(functools.partial(fused, groups, quarters), out_shape=(jax...]
    unnamed x15 -> x13, local copies, waits for them, and re-layouts: 6.61 us -> 6.52 us
where the time goes in v3:
time: 95.2 us; the launch traced here: 94.8 us
  Pallas kernels  87.6 us (92%)
  local copies, waits for them, and re-layouts  6.52 us (7%)
    pallas_call x1, Pallas kernels, by_feature(): pl.pallas_call(functools.partial(fused, groups, quarters), out_shape=(jax...  87.6 us
    unnamed x13, local copies, waits for them, and re-layouts  6.52 us

profile of v3, /device:TPU:0, one launch (start us, length us, event | category | flops | bytes accessed | tf_op | source)
XLA Modules:
  0.0 94.8 jit_solution(183440177509887701)
XLA Ops:
  0.6 0.0 copy-start.2
  0.6 0.8 copy.11
  1.5 0.8 copy.13
  2.3 0.0 copy-start.3
  2.3 0.0 copy-done.2
  2.3 0.7 copy-done.3
  3.0 0.0 copy-start
  3.0 1.0 %copy-done = bf16[512,512]{1,0:T(8,128)(2,1)S(1)} copy-done((bf16[512,512]{1,0:T(8,128)(2,1)S(1)}, bf16[512,512]{1,0:T(8,128)(2,1)}, u32[]{:S(2)}) %copy-start) | copy-done | bytes 524312
  4.0 0.0 copy-start.1
  4.0 0.9 %copy-done.1 = bf16[2,64,1024]{2,1,0:T(8,128)(2,1)S(1)} copy-done((bf16[2,64,1024]{2,1,0:T(8,128)(2,1)S(1)}, bf16[2,64,1024]{2,1,0:T(8,128)(2,1)}, u32[]{:S(2)}) %copy-start.1) | copy-done | bytes 262168
  5.0 87.6 %shard_map.85 = (bf16[2,64,512]{2,1,0:T(8,128)(2,1)S(1)}, f32[512,512]{1,0:T(8,128)S(1)}, f32[8,1,128]{2,1,0:T(1,128)S(1)}) custom-call(bf16[2,64,512]{2,1,0:T(8,128)(2,1)S(1)} %copy-done.2, bf16[2,64,1024]{2,1,0:T(8,128)(2,1)S(1)} %copy-done.1, bf16[512,512]{1,0:T(8,128)(2,1)S(1)} %copy-done, f32[8,128]{1,0:T(8,128)S(1)} %bitcast.2, ...), custom_call_target="tpu_custom_call" | custom-call | tf_op jit(solution)/shard_map/pallas_call | solution.py:558
  92.6 0.7 copy.17
  93.2 1.0 %copy.18 = f32[512,512]{1,0:T(8,128)} copy(f32[512,512]{1,0:T(8,128)S(1)} %get-tuple-element.13) | data formatting | bytes 2097152
  94.2 0.6 copy.19
  (1 shorter events, 0.0 us)
Async XLA Ops:
  0.6 1.7 %copy-start.2 = (bf16[2,64,512]{2,1,0:T(8,128)(2,1)S(1)}, bf16[2,64,512]{2,1,0:T(8,128)(2,1)}, u32[]{:S(2)}) copy-start(bf16[2,64,512]{2,1,0:T(8,128)(2,1)} %attn.1) | copy-start | bytes 393220
  2.3 0.7 copy-start.3
  3.0 1.0 %copy-start = (bf16[512,512]{1,0:T(8,128)(2,1)S(1)}, bf16[512,512]{1,0:T(8,128)(2,1)}, u32[]{:S(2)}) copy-start(bf16[512,512]{1,0:T(8,128)(2,1)} %w_hbm.1) | copy-start | bytes 1572868
  4.0 0.9 %copy-start.1 = (bf16[2,64,1024]{2,1,0:T(8,128)(2,1)S(1)}, bf16[2,64,1024]{2,1,0:T(8,128)(2,1)}, u32[]{:S(2)}) copy-start(bf16[2,64,1024]{2,1,0:T(8,128)(2,1)} %resid.1) | copy-start | bytes 786436
